TPU v7x, 256 devices: a whole 4x4x8 slice. The times are simulated.
256 devices in a mesh: aux: 64 (over z, x, core), pair: 4 (over y).
Axes of the slice: x: 4, y: 4, z: 8, core: 2. Of those that a mesh axis runs over, the one named last changes fastest.
Arguments:
- three_center: float32 [65536, 4, 384], P('aux', 'pair'), may hold values from -1 to 1
- occ_energy: float32 [4], P('pair'), may hold values from -1.5 to -0.3
- vir_energy: float32 [384], replicated, may hold values from 0.2 to 3
- pair_mask: int32 [4, 4], replicated, may hold values from 0 to 1, as said below
Outputs:
- gamma_aux: float32 [65536, 4, 384], P('aux', 'pair')
Inputs may be any that keep to these rules, and one draw needn't show every extreme that they name: pair_mask is symmetric and holds 1 on its diagonal.
All inputs are finite; a program needn't handle non-finite values.
Results may differ from a plain program's by a relative error of at most 0.000071.
Values sent between devices are 32-bit elements; how exact they have to be, the bound alone decides.
A program may use at most 64 MiB of HBM per device.

v0:
```python
import jax
import jax.numpy as jnp
from jax import lax
from jax.sharding import PartitionSpec as P

highest = lax.Precision.HIGHEST


def from_behind(value, axis, by):
    peers = lax.axis_size(axis)
    return lax.ppermute(value, axis, [(i, (i + by) % peers) for i in range(peers)])


def contract_columns(stationary_part, moving):
    return lax.dot_general(
        stationary_part,
        moving,
        (((0,), (0,)), ((), ())),
        precision=highest,
        preferred_element_type=jnp.float32,
    )


def back_product(visitor, piece_rows):
    return lax.dot_general(
        visitor,
        piece_rows,
        (((1,), (1,)), ((), ())),
        precision=highest,
        preferred_element_type=jnp.float32,
    )


def amplitude_block(int_slab, first_row, row_occ, col_occ, vir_energy, mask_side):
    row_total, flat_width = int_slab.shape
    virt_count = vir_energy.shape[0]
    occ_count = row_occ.shape[0]
    row_ids = first_row + jnp.arange(row_total, dtype=jnp.int32)
    occ_pick = (
        row_ids[:, None] // virt_count == jnp.arange(occ_count, dtype=jnp.int32)[None, :]
    ).astype(jnp.float32)
    vir_pick = (
        row_ids[:, None] % virt_count == jnp.arange(virt_count, dtype=jnp.int32)[None, :]
    ).astype(jnp.float32)
    row_term = jnp.dot(vir_pick, vir_energy, precision=highest) - jnp.dot(
        occ_pick, row_occ, precision=highest
    )
    col_term = vir_energy[None, :] - col_occ[:, None]
    mask_rows = jnp.dot(occ_pick, mask_side.astype(jnp.float32), precision=highest)
    denominator = row_term[:, None, None] + col_term[None, :, :]
    values = (
        mask_rows[:, :, None] * int_slab.reshape(row_total, occ_count, virt_count) / denominator
    )
    return values.reshape(row_total, flat_width)


def on_device(three_center, occ_energy, vir_energy, pair_mask):
    aux_local, occ_count, virt_count = three_center.shape
    flat_width = occ_count * virt_count
    pair_count = lax.axis_size("pair")
    aux_count = lax.axis_size("aux")
    pair_index = lax.axis_index("pair")
    slab_rows = flat_width // aux_count
    first_row = lax.axis_index("aux") * slab_rows
    resident = three_center.reshape(aux_local, flat_width)
    gamma_aux = jnp.zeros((aux_local, flat_width), jnp.float32)
    visitor, visitor_occ = (resident, occ_energy)
    for offset in range(pair_count):
        source = (pair_index - offset) % pair_count
        if offset > 0:
            visitor, visitor_occ = from_behind((visitor, visitor_occ), "pair", 1)
        block_mask = lax.dynamic_slice(
            pair_mask, (pair_index * occ_count, source * occ_count), (occ_count, occ_count)
        )
        block_live = jnp.any(block_mask > 0)
        stationary, moving = (resident, visitor)
        row_occ, col_occ, mask_side = (occ_energy, visitor_occ, block_mask)

        def partial_ints(
            row_start, row_total, stationary=stationary, moving=moving, block_live=block_live
        ):
            return contract_columns(stationary, moving)

        int_slab = lax.psum_scatter(
            partial_ints(jnp.int32(0), slab_rows * lax.axis_size("aux")),
            "aux",
            scatter_dimension=0,
            tiled=True,
        )
        amplitudes = amplitude_block(int_slab, first_row, row_occ, col_occ, vir_energy, mask_side)

        def spread(piece_rows, row_start, moving=moving, block_live=block_live):
            return back_product(moving, piece_rows)

        gamma_aux = gamma_aux + spread(
            lax.all_gather(amplitudes, "aux", axis=0, tiled=True), jnp.int32(0)
        )
    return gamma_aux.reshape(aux_local, occ_count, virt_count)


def solution(mesh):
    in_specs = (P("aux", "pair", None), P("pair"), P(), P())
    out_specs = P("aux", "pair", None)
    return jax.shard_map(
        on_device, mesh=mesh, in_specs=in_specs, out_specs=out_specs, check_vma=False
    )
```

profile of v0, /device:TPU:1, one launch (start us, length us, event | category | flops | bytes accessed | tf_op | source)
XLA Modules:
  0.0 562.0 jit_solution(5788302358518271166)
XLA Ops:
  6.5 0.0 all-reduce.7.cloned.1.call-start
  6.5 1.6 copy.15
  8.2 2.2 collective-permute-start
  10.4 33.5 %collective-permute-done = f32[1024,384]{1,0:T(8,128)S(1)} collective-permute-done((f32[1024,384]{1,0:T(8,128)S(1)}, f32[1024,384]{1,0:T(8,128)S(1)}, u32[]{:S(2)}, u32[]{:S(2)}) %collective-permute-start) | collective-permute-done | bytes 1572896 | tf_op jit(solution)/shard_map/ppermute | solution.py:11
  43.9 1.6 collective-permute-start.2
  45.4 33.3 %collective-permute-done.2 = f32[1024,384]{1,0:T(8,128)S(1)} collective-permute-done((f32[1024,384]{1,0:T(8,128)S(1)}, f32[1024,384]{1,0:T(8,128)S(1)}, u32[]{:S(2)}, u32[]{:S(2)}) %collective-permute-start.2) | collective-permute-done | bytes 1572896 | tf_op jit(solution)/shard_map/ppermute | solution.py:11
  78.7 1.3 collective-permute-start.4
  80.0 0.0 copy-done
  80.0 3.5 fusion.16
  83.6 3.5 fusion.14
  87.1 0.0 copy-done.1
  87.1 3.5 fusion.13
  90.6 22.1 %collective-permute-done.4 = f32[1024,384]{1,0:T(8,128)S(1)} collective-permute-done((f32[1024,384]{1,0:T(8,128)S(1)}, f32[1024,384]{1,0:T(8,128)S(1)}, u32[]{:S(2)}, u32[]{:S(2)}) %collective-permute-start.4) | collective-permute-done | bytes 1572896 | tf_op jit(solution)/shard_map/ppermute | solution.py:11
  112.6 1.2 copy-done.3
  113.8 3.5 fusion.12
  117.3 0.0 all-reduce.7.cloned.1.call-update
  117.3 0.9 collective-permute-start.1
  119.0 0.0 copy-done.9
  119.0 0.7 fusion.17
  120.9 0.0 copy-done.8
  122.2 0.0 copy-done.10
  122.2 0.6 dynamic-slice
  123.6 0.2 fusion
  123.8 0.0 collective-permute-done.1
  123.8 1.9 collective-permute-start.3
  125.7 1.9 collective-permute-done.3
  127.6 0.7 collective-permute-start.5
  128.3 3.1 collective-permute-done.5
  131.4 1.9 broadcast_subtract_fusion
  133.3 179.6 %all-reduce.7.cloned.1.call-done = (f32[384,384]{1,0:T(8,128)}, f32[384,384]{1,0:T(8,128)}, f32[384,384]{1,0:T(8,128)}, f32[384,384]{1,0:T(8,128)}) async-done(((f32[384,384]{1,0:T(8,128)}, f32[384,384]{1,0:T(8,128)}, f32[384,384]{1,0:T(8,128)}, f32[384,384]{1,0:T(8,128)}), (f32[384,384]{1,0:T(8,128)}, f32[384,384]{1,0:T(8,128)}, f32[384,384]{1,0:T(8,128)}, ...) | async-done | bytes 2359312
  312.9 0.9 fusion.2
  313.8 55.6 %all-gather.2 = f32[64,6,384]{2,1,0:T(8,128)} all-gather(f32[1,6,384]{2,1,0:T(8,128)S(1)} %get-tuple-element.18), channel_id=1, replica_groups=mesh['aux'=64,'pair'=4] {'aux'}, dimensions={0}, use_global_device_ids=true | all-gather | bytes 599040 | tf_op jit(solution)/shard_map/all_gather | solution.py:96
  369.4 2.0 reshape.143
  371.4 53.2 %all-gather = f32[64,6,384]{2,1,0:T(8,128)} all-gather(f32[1,6,384]{2,1,0:T(8,128)S(1)} %get-tuple-element.20), channel_id=1, replica_groups=mesh['aux'=64,'pair'=4] {'aux'}, dimensions={0}, use_global_device_ids=true | all-gather | bytes 599040 | tf_op jit(solution)/shard_map/all_gather | solution.py:96
  424.6 2.0 reshape.139
  426.7 4.9 fusion.15
  431.6 53.1 %all-gather.1 = f32[64,6,384]{2,1,0:T(8,128)} all-gather(f32[1,6,384]{2,1,0:T(8,128)S(1)} %get-tuple-element.19), channel_id=1, replica_groups=mesh['aux'=64,'pair'=4] {'aux'}, dimensions={0}, use_global_device_ids=true | all-gather | bytes 599040 | tf_op jit(solution)/shard_map/all_gather | solution.py:96
  484.7 2.2 reshape.141
  486.8 53.7 %all-gather.3 = f32[64,6,384]{2,1,0:T(8,128)} all-gather(f32[1,6,384]{2,1,0:T(8,128)S(1)} %get-tuple-element.17), channel_id=1, replica_groups=mesh['aux'=64,'pair'=4] {'aux'}, dimensions={0}, use_global_device_ids=true | all-gather | bytes 599040 | tf_op jit(solution)/shard_map/all_gather | solution.py:96
  540.5 2.1 reshape.145
  542.6 0.0 copy-done.2
  542.6 3.8 fusion.19
  546.4 0.0 copy-done.7
  546.4 0.0 copy-start.4
  546.4 0.0 copy-start.5
  546.5 2.7 fusion.18
  549.2 2.9 add_bitcast_fusion
  552.2 2.7 copy.7
  (16 shorter events, 0.1 us)
Async XLA Ops:
  6.5 73.5 %copy-start = (f32[1024,1,384]{2,1,0:T(1,128)S(1)}, f32[1024,1,384]{2,1,0:T(1,128)}, u32[]{:S(2)}) copy-start(f32[1024,1,384]{2,1,0:T(1,128)} %param.4) | copy-start | bytes 4718596
  6.5 306.4 %all-reduce.7.cloned.1.call-start = ((), (), s32[]{:S(2)}) async-start(), calls=%async_computation | async-start | bytes 4718592
  8.2 35.7 %collective-permute-start = (f32[1024,384]{1,0:T(8,128)S(1)}, f32[1024,384]{1,0:T(8,128)S(1)}, u32[]{:S(2)}, u32[]{:S(2)}) collective-permute-start(f32[1024,384]{1,0:T(8,128)S(1)} %bitcast.46), channel_id=1, source_target_pairs={{0,1},{1,2},{2,3},{3,0},{4,5},{5,6},{6,7},{7,4},{8,9},{9,10},{10,1... | collective-permute-start | bytes 4718600 | tf_op jit(solution)/shard_map/ppermute | solution.py:11
  43.9 34.8 %collective-permute-start.2 = (f32[1024,384]{1,0:T(8,128)S(1)}, f32[1024,384]{1,0:T(8,128)S(1)}, u32[]{:S(2)}, u32[]{:S(2)}) collective-permute-start(f32[1024,384]{1,0:T(8,128)S(1)} %collective-permute-done), channel_id=1, source_target_pairs={{0,1},{1,2},{2,3},{3,0},{4,5},{5,6},{6,7},{7,4},{8,9},{9,10},{10,1... | collective-permute-start | bytes 4718600 | tf_op jit(solution)/shard_map/ppermute | solution.py:11
  78.7 8.3 %copy-start.1 = (f32[1024,384]{1,0:T(8,128)}, f32[1024,384]{1,0:T(8,128)S(1)}, u32[]{:S(2)}) copy-start(f32[1024,384]{1,0:T(8,128)S(1)} %collective-permute-done.2) | copy-start | bytes 4718596
  78.7 33.9 %collective-permute-start.4 = (f32[1024,384]{1,0:T(8,128)S(1)}, f32[1024,384]{1,0:T(8,128)S(1)}, u32[]{:S(2)}, u32[]{:S(2)}) collective-permute-start(f32[1024,384]{1,0:T(8,128)S(1)} %collective-permute-done.2), channel_id=1, source_target_pairs={{0,1},{1,2},{2,3},{3,0},{4,5},{5,6},{6,7},{7,4},{8,9},{9,10},{10,1... | collective-permute-start | bytes 4718600 | tf_op jit(solution)/shard_map/ppermute | solution.py:11
  112.6 1.2 copy-start.3
  117.3 1.7 copy-start.9
  117.3 3.6 copy-start.8
  117.3 4.9 copy-start.10
  117.3 6.5 %collective-permute-start.1 = (f32[1]{0:T(128)}, f32[1]{0:T(128)}, u32[]{:S(2)}, u32[]{:S(2)}) collective-permute-start(f32[1]{0:T(128)} %param.5), channel_id=1, source_target_pairs={{0,1},{1,2},{2,3},{3,0},{4,5},{5,6},{6,7},{7,4},{8,9},{9,10},{10,1... | collective-permute-start | bytes 20 | tf_op jit(solution)/shard_map/ppermute | solution.py:11
  123.8 3.8 collective-permute-start.3
  127.6 3.8 collective-permute-start.5
  484.7 57.9 %copy-start.2 = (f32[1024,384]{1,0:T(8,128)S(1)}, f32[1024,384]{1,0:T(8,128)}, u32[]{:S(2)}) copy-start(f32[1024,384]{1,0:T(8,128)} %copy-done.1) | copy-start | bytes 4718596
  542.6 3.8 copy-start.7
  546.4 2.8 copy-start.4
  546.4 2.8 copy-start.5
  546.5 2.8 copy-start.6
Sparse Core Ops, SparseCore 0:
  117.5 195.4 all-reduce.6
where the time goes:
time: 565 us; the launch traced here: 562 us
  waiting for transfers between devices  274 us (48%)
  blocking collectives  216 us (38%)
  matrix products  28.6 us (5%)
  between operations  17.7 us (3%)
  local copies, waits for them, and re-layouts  15.2 us (3%)
  starting transfers between devices  8.54 us (2%)
    all_gather x4, blocking collectives, on_device(): lax.all_gather(amplitudes, 'aux', axis=0, tiled=True)  216 us
    unnamed x2, waiting for transfers between devices  180 us
    ppermute x6, waiting for transfers between devices, from_behind(): lax.ppermute(value, axis, [(i, (i + by) % peers) for i in range(peers)])  93.9 us
    dot_general x4, matrix products, back_product(): lax.dot_general(visitor, piece_rows, (((1,), (1,)), ((), ())), precision=...  14.4 us
    dot_general x4, matrix products, contract_columns(): lax.dot_general(stationary_part, moving, (((0,), (0,)), ((), ())), precis...  14.1 us
    unnamed x29, local copies, waits for them, and re-layouts  11.8 us
  transfers between devices with their start and end apart: 7, of which 6 were waited for; matrix products, arithmetic and copies ran while one was open for 2% of the time, Pallas kernels for 0%

commit v1 on v0

v1 whole, which is shorter than its diff:
```python
import functools

import jax
import jax.numpy as jnp
from jax import lax
from jax.experimental import pallas as pl
from jax.experimental.pallas import tpu as pltpu
from jax.sharding import PartitionSpec as P

MESH = pl.DeviceIdType.MESH
f32 = jnp.float32
bf16 = jnp.bfloat16

NQ = 1024
V = 384
QT = 256
OWNERS = 6


def split(value):
    high = value.astype(bf16)
    return high, (value - high.astype(f32)).astype(bf16)


def gram(left, right):
    return lax.dot_general(
        left, right, (((0,), (0,)), ((), ())), preferred_element_type=f32
    )


def kernel(
    own, occ, vir, mask, out,
    nb, hp, lp, part, r1, r2, r3, r4, tot, amp, ah, al, acc, oc, vcol,
    bs, br, os_, or_, js, jr,
):
    y = lax.axis_index("pair")
    aux = lax.axis_index("aux")
    core = lax.rem(aux, 2)
    x = lax.rem(aux // 2, 4)
    z = aux // 8
    up, down, far = (lax.rem(y + d, 4) for d in (1, 3, 2))

    def at_x(d):
        return {"aux": (z * 4 + lax.rem(x + d, 4)) * 2 + core}

    def at_z(d):
        return {"aux": (lax.rem(z + d, 8) * 4 + x) * 2 + core}

    sibling = {"aux": aux + 1 - 2 * core}

    def remote(src, dst, send, recv, device):
        return pltpu.make_async_remote_copy(
            src, dst, send, recv, device_id=device, device_id_type=MESH
        )

    def wait_bytes(ref, sem):
        pltpu.make_async_copy(ref, ref, sem).wait()

    barrier = pltpu.get_barrier_semaphore()
    partners = [{"pair": t} for t in (up, down, far)]
    partners += [at_x(d) for d in (1, 2, 3)] + [at_z(d) for d in range(1, 8)] + [sibling]
    for partner in partners:
        pl.semaphore_signal(barrier, 1, device_id=partner, device_id_type=MESH)
    pl.semaphore_wait(barrier, len(partners))

    oc[y] = jnp.full((8, 128), occ[0], f32)
    for i, t in enumerate((up, down, far)):
        remote(oc.at[y], oc.at[y], os_.at[i], or_.at[0], {"pair": t}).start()

    def wanted(node):
        return lax.rem(node, 4) // 2

    def bulk(k, direction):
        if direction == 0:
            first, relay = wanted(y + 2), wanted(y + 1)
            src, dst, q = (
                (own, 0, first), (own, 0, 1 - first), (nb.at[0], 2, relay),
                (own, 0, 2), (own, 0, 3), (nb.at[0], 2, 1 - relay),
            )[k]
        else:
            first, relay = 2 + wanted(y + 2), 2 + wanted(y + 3)
            src, dst, q = (
                (own, 1, first), (own, 1, 5 - first), (nb.at[1], 2, relay),
                (own, 1, 0), (own, 1, 1), (nb.at[1], 2, 5 - relay),
            )[k]
        rows = pl.ds(pl.multiple_of(q * (3 * QT), 8), 3 * QT)
        return remote(
            src.at[rows], nb.at[dst, rows], bs.at[direction, k], br.at[direction, k],
            {"pair": up if direction == 0 else down},
        )

    def send(k):
        for d in (0, 1):
            bulk(k, d).start()

    def arrive(k):
        for d in (0, 1):
            bulk(k, d).wait_recv()

    def convert(slot, src, q):
        block = src.at[pl.ds(pl.multiple_of(q * (3 * QT), 8), 3 * QT)]
        rows = pl.ds(pl.multiple_of(q * QT, QT), QT)
        for c in range(3):
            high, low = split(block[pl.ds(c, QT, stride=3), :])
            hp[slot, rows, c * 128 : (c + 1) * 128] = high
            lp[slot, rows, c * 128 : (c + 1) * 128] = low

    def contract(t, left, right, q, first):
        rows = pl.ds(pl.multiple_of(q * QT, QT), QT)
        lh, ll, rh, rl = hp[left, rows], lp[left, rows], hp[right, rows], lp[right, rows]
        value = gram(lh, rh) + gram(lh, rl) + gram(ll, rh)
        part[t] = value if first else part[t] + value

    half = pl.multiple_of(core * 192, 8)
    other = pl.multiple_of((1 - core) * 192, 8)
    mine_x = pl.multiple_of(half + x * 48, 8)
    mine = pl.multiple_of(mine_x + z * 8, 8)
    jobs = {"D": (0, 0, 1), "E": (1, 1, 2), "F": (2, 3, 1)}
    owner = z < OWNERS

    def core_sum(name, begin):
        j, b, n = jobs[name]
        copy = remote(
            part.at[pl.ds(b, n), pl.ds(other, 192)], r1.at[pl.ds(b, n)], js.at[j, 0], jr.at[j, 0], sibling
        )
        if begin:
            copy.start()
        else:
            copy.wait_recv()
            part[b : b + n, pl.ds(half, 192)] += r1[b : b + n]

    def x_sum(name, begin):
        j, b, n = jobs[name]
        if begin:
            for d in (2, 1, 3):
                rows = pl.ds(pl.multiple_of(half + lax.rem(x + d, 4) * 48, 8), 48)
                remote(
                    part.at[pl.ds(b, n), rows], r2.at[d - 1, pl.ds(b, n)], js.at[j, 1], jr.at[j, 1], at_x(d)
                ).start()
        else:
            wait_bytes(r2.at[:, pl.ds(b, n)], jr.at[j, 1])
            part[b : b + n, pl.ds(mine_x, 48)] += (
                r2[0, b : b + n] + r2[1, b : b + n] + r2[2, b : b + n]
            )

    def z_sum(name, begin):
        j, b, n = jobs[name]
        if begin:
            for d in (4, 3, 5, 2, 6, 1, 7):
                zd = lax.rem(z + d, 8)

                @pl.when(zd < OWNERS)
                def _():
                    rows = pl.ds(pl.multiple_of(mine_x + zd * 8, 8), 8)
                    remote(
                        part.at[pl.ds(b, n), rows], r3.at[d - 1, pl.ds(b, n)], js.at[j, 2], jr.at[j, 2], at_z(d)
                    ).start()
        else:

            @pl.when(owner)
            def _():
                wait_bytes(r3.at[:, pl.ds(b, n)], jr.at[j, 2])
                value = part[b : b + n, pl.ds(mine, 8)]
                for d in range(7):
                    value += r3[d, b : b + n]
                tot[b : b + n] = value

    def y_sum(name, begin):
        j = jobs[name][0]
        moves = {"E": ((1, 2, down, 3), (2, 1, up, 4)), "F": ((3, 3, far, 3),)}[name]

        @pl.when(owner)
        def _():
            for src, dst, t, s in moves:
                copy = remote(tot.at[src], r4.at[dst], js.at[j, s], jr.at[j, s], {"pair": t})
                if begin:
                    copy.start()
                else:
                    copy.wait_recv()

    low_far = lax.rem(y, 2)
    sides = {0: (y, y), 1: (down, y), 2: (y, up), 3: (low_far, low_far + 2)}

    def scale(name):
        _, b, n = jobs[name]

        @pl.when(owner)
        def _():
            for t in range(b, b + n):
                p, r = sides[t]
                denominator = (vcol[pl.ds(mine, 8), 0:1] + vir[...]) - oc[p, 0:1, 0:1] - oc[r, 0:1, 0:1]
                weight = mask[p, r].astype(f32)
                total = tot[t] + r4[t] if t else tot[t]
                amp[t, pl.ds(mine, 8)] = (weight * total) / denominator

    def z_gather(name, begin):
        j, b, n = jobs[name]
        if begin:

            @pl.when(owner)
            def _():
                ref = amp.at[pl.ds(b, n), pl.ds(mine, 8)]
                for d in (4, 3, 5, 2, 6, 1, 7):
                    remote(ref, ref, js.at[j, 5], jr.at[j, 5], at_z(d)).start()
        else:

            @pl.when(owner)
            def _():
                wait_bytes(amp.at[pl.ds(b, n), pl.ds(mine_x, 40)], jr.at[j, 5])

            @pl.when(jnp.logical_not(owner))
            def _():
                wait_bytes(amp.at[pl.ds(b, n), pl.ds(mine_x, 48)], jr.at[j, 5])

    def x_gather(name, begin):
        j, b, n = jobs[name]
        if begin:
            ref = amp.at[pl.ds(b, n), pl.ds(mine_x, 48)]
            for d in (2, 1, 3):
                remote(ref, ref, js.at[j, 6], jr.at[j, 6], at_x(d)).start()
        else:
            wait_bytes(amp.at[pl.ds(b, n), pl.ds(half, 144)], jr.at[j, 6])

    def core_gather(name, begin):
        j, b, n = jobs[name]
        ref = amp.at[pl.ds(b, n), pl.ds(half, 192)]
        copy = remote(ref, ref, js.at[j, 7], jr.at[j, 7], sibling)
        if begin:
            copy.start()
        else:
            wait_bytes(amp.at[pl.ds(b, n), pl.ds(other, 192)], jr.at[j, 7])

    def factor(slot, turned):
        value = amp[slot]
        ah[slot], al[slot] = split(value.T if turned else value)

    def back(slot, rows):
        high = hp[slot, rows]
        value = jnp.dot(high, ah[slot], preferred_element_type=f32)
        value += jnp.dot(high, al[slot], preferred_element_type=f32)
        return value + jnp.dot(lp[slot, rows], ah[slot], preferred_element_type=f32)

    def quarters(body):
        def step(q, carry):
            body(q, pl.ds(pl.multiple_of(q * QT, QT), QT))
            return carry

        lax.fori_loop(0, 4, step, 0)

    q_far = wanted(y)

    send(0)
    send(1)
    vcol[...] = jnp.broadcast_to(vir[...], (128, V)).T

    part[0] = jnp.zeros((V, V), f32)

    def own_step(q, rows):
        convert(0, own, q)
        contract(0, 0, 0, q, False)

    quarters(own_step)
    core_sum("D", True)
    wait_bytes(oc.at[pl.ds(0, 3)], or_.at[0])
    core_sum("D", False)
    x_sum("D", True)
    arrive(0)
    send(2)
    x_sum("D", False)
    z_sum("D", True)
    first_up, first_down = wanted(y + 1), 2 + wanted(y + 3)
    convert(1, nb.at[0], first_up)
    convert(2, nb.at[1], first_down)
    contract(1, 1, 0, first_up, True)
    contract(2, 0, 2, first_down, True)
    z_sum("D", False)
    scale("D")
    z_gather("D", True)
    arrive(1)
    send(3)
    convert(1, nb.at[0], 1 - first_up)
    convert(2, nb.at[1], 5 - first_down)
    contract(1, 1, 0, 1 - first_up, False)
    contract(2, 0, 2, 5 - first_down, False)
    core_sum("E", True)
    z_gather("D", False)
    x_gather("D", True)
    core_sum("E", False)
    x_sum("E", True)
    x_gather("D", False)
    core_gather("D", True)
    arrive(2)
    send(4)
    convert(3, nb.at[2], q_far)
    convert(3, nb.at[2], 2 + q_far)
    left = jnp.where(y < 2, 0, 3)
    contract(3, left, 3 - left, q_far, True)
    contract(3, left, 3 - left, 2 + q_far, False)
    core_sum("F", True)
    x_sum("E", False)
    z_sum("E", True)
    core_sum("F", False)
    x_sum("F", True)
    core_gather("D", False)
    factor(0, False)

    def own_back(q, rows):
        acc[rows] = back(0, rows)

    quarters(own_back)
    z_sum("E", False)
    y_sum("E", True)
    x_sum("F", False)
    z_sum("F", True)
    arrive(3)
    convert(1, nb.at[0], 2)
    convert(2, nb.at[1], 0)
    y_sum("E", False)
    scale("E")
    z_gather("E", True)
    z_sum("F", False)
    y_sum("F", True)
    send(5)
    arrive(4)
    convert(1, nb.at[0], 3)
    convert(2, nb.at[1], 1)
    y_sum("F", False)
    scale("F")
    z_gather("F", True)
    z_gather("E", False)
    x_gather("E", True)
    z_gather("F", False)
    x_gather("F", True)
    x_gather("E", False)
    core_gather("E", True)
    arrive(5)
    convert(3, nb.at[2], 1 - q_far)
    convert(3, nb.at[2], 3 - q_far)
    core_gather("E", False)
    factor(1, False)
    factor(2, True)

    def near_back(q, rows):
        acc[rows] += back(1, rows) + back(2, rows)

    quarters(near_back)
    x_gather("F", False)
    core_gather("F", True)
    core_gather("F", False)

    @pl.when(y < 2)
    def _():
        factor(3, True)

    @pl.when(y >= 2)
    def _():
        factor(3, False)

    def far_back(q, rows):
        value = acc[rows] + back(3, rows)
        block = out.at[pl.ds(pl.multiple_of(q * (3 * QT), 8), 3 * QT)]
        for c in range(3):
            block[pl.ds(c, QT, stride=3), :] = value[:, c * 128 : (c + 1) * 128]

    quarters(far_back)

    for k in range(6):
        for d in (0, 1):
            bulk(k, d).wait_send()
    for i in range(3):
        wait_bytes(oc.at[0], os_.at[i])
    for name, (j, b, n) in jobs.items():
        blocks = pl.ds(b, n)
        wait_bytes(r1.at[blocks], js.at[j, 0])
        wait_bytes(r2.at[:, blocks], js.at[j, 1])
        wait_bytes(r2.at[:, blocks], js.at[j, 6])
        wait_bytes(r1.at[blocks], js.at[j, 7])

        @pl.when(owner)
        def _():
            wait_bytes(r3.at[pl.ds(0, OWNERS - 1), blocks], js.at[j, 2])
            wait_bytes(r3.at[:, blocks], js.at[j, 5])
            for s in range(3, 3 + {"D": 0, "E": 2, "F": 1}[name]):
                wait_bytes(tot.at[0], js.at[j, s])

        @pl.when(jnp.logical_not(owner))
        def _():
            wait_bytes(r3.at[pl.ds(0, OWNERS), blocks], js.at[j, 2])


def on_device(three_center, occ_energy, vir_energy, pair_mask):
    flat = three_center.reshape(3 * NQ, 128)
    vmem = pl.BlockSpec(memory_space=pltpu.VMEM)
    smem = pl.BlockSpec(memory_space=pltpu.SMEM)
    dma = pltpu.SemaphoreType.DMA
    result = pl.pallas_call(
        kernel,
        out_shape=jax.ShapeDtypeStruct((3 * NQ, 128), f32),
        in_specs=[vmem, smem, vmem, smem],
        out_specs=vmem,
        scratch_shapes=[
            pltpu.VMEM((3, 3 * NQ, 128), f32),
            pltpu.VMEM((4, NQ, V), bf16),
            pltpu.VMEM((4, NQ, V), bf16),
            pltpu.VMEM((4, V, V), f32),
            pltpu.VMEM((4, 192, V), f32),
            pltpu.VMEM((3, 4, 48, V), f32),
            pltpu.VMEM((7, 4, 8, V), f32),
            pltpu.VMEM((4, 8, V), f32),
            pltpu.VMEM((4, 8, V), f32),
            pltpu.VMEM((4, V, V), f32),
            pltpu.VMEM((4, V, V), bf16),
            pltpu.VMEM((4, V, V), bf16),
            pltpu.VMEM((NQ, V), f32),
            pltpu.VMEM((4, 8, 128), f32),
            pltpu.VMEM((V, 128), f32),
            dma((2, 6)),
            dma((2, 6)),
            dma((3,)),
            dma((1,)),
            dma((3, 8)),
            dma((3, 8)),
        ],
        compiler_params=pltpu.CompilerParams(
            collective_id=0, has_side_effects=True, vmem_limit_bytes=48 << 20
        ),
    )(flat, occ_energy, vir_energy.reshape(1, V), pair_mask)
    return result.reshape(NQ, 1, V)


def solution(mesh):
    in_specs = (P("aux", "pair", None), P("pair"), P(), P())
    out_specs = P("aux", "pair", None)
    return jax.shard_map(
        on_device, mesh=mesh, in_specs=in_specs, out_specs=out_specs, check_vma=False
    )
```

time: 565 us -> 83.5 us (0.15)
  waiting for transfers between devices: 274 us -> 0 us
  blocking collectives: 216 us -> 0 us
  Pallas kernels: 0 us -> 78.8 us
  matrix products: 28.6 us -> 0 us
  between operations: 17.7 us -> 0.66 us
  local copies, waits for them, and re-layouts: 15.2 us -> 3.92 us
  starting transfers between devices: 8.54 us -> 0 us
    all_gather x4 -> x0, blocking collectives: 216 us -> none  [on_device(): lax.all_gather(amplitudes, 'aux', axis=0, tiled=True)]
    unnamed x2 -> x0, waiting for transfers between devices: 180 us -> none
    ppermute x6 -> x0, waiting for transfers between devices: 93.9 us -> none  [from_behind(): lax.ppermute(value, axis, [(i, (i + by) % peers) for i in range(peers)])]
    pallas_call x0 -> x1, Pallas kernels: none -> 78.8 us  [on_device(): pl.pallas_call(kernel, out_shape=jax.ShapeDtypeStruct((3 * NQ, 128), f32)...]
    dot_general x9 -> x0, matrix products: 28.6 us -> none  [the longest x4 14.4 us: back_product(): lax.dot_general(visitor, piece_rows, (((1,), (1,)), ((), ())), precision=...]
    unnamed x29 -> x5, local copies, waits for them, and re-layouts: 11.8 us -> 3.23 us
    ppermute x6 -> x0, starting transfers between devices: 8.54 us -> none  [from_behind(): lax.ppermute(value, axis, [(i, (i + by) % peers) for i in range(peers)])]
  transfers between devices with their start and end apart: 7 -> 0, of which waited for: 6 -> 0; matrix products, arithmetic and copies ran while one was open for 2% -> 0% of each run, Pallas kernels for 0% -> 0%
where the time goes in v1:
time: 83.5 us; the launch traced here: 83.3 us
  Pallas kernels  78.8 us (94%)
  local copies, waits for them, and re-layouts  3.92 us (5%)
    pallas_call x1, Pallas kernels, on_device(): pl.pallas_call(kernel, out_shape=jax.ShapeDtypeStruct((3 * NQ, 128), f32)...  78.8 us
    unnamed x5, local copies, waits for them, and re-layouts  3.23 us

profile of v1, /device:TPU:1, one launch (start us, length us, event | category | flops | bytes accessed | tf_op | source)
XLA Modules:
  0.0 83.3 jit_solution(5742755386022466605)
XLA Ops:
  0.7 0.7 reshape.10.vir
  1.3 0.0 copy-start
  1.3 1.4 %copy-done = f32[1024,1,384]{2,1,0:T(1,128)S(1)} copy-done((f32[1024,1,384]{2,1,0:T(1,128)S(1)}, f32[1024,1,384]{2,1,0:T(1,128)}, u32[]{:S(2)}) %copy-start) | copy-done | bytes 1572888
  2.7 0.0 copy-start.1
  2.7 0.7 copy-done.1
  3.4 78.8 %shard_map.46 = f32[3072,128]{1,0:T(8,128)S(1)} custom-call(f32[3072,128]{1,0:T(8,128)S(1)} %bitcast.3, f32[1]{0:T(128)S(6)} %copy.7.occ, f32[1,384]{1,0:T(1,128)S(1)} %reshape.10.vir, s32[4,4]{1,0:T(4,128)S(1)} %copy-done.1), custom_call_target="tpu_custom_call" | custom-call | tf_op jit(solution)/shard_map/pallas_call | solution.py:396
  82.2 1.1 %copy.8 = f32[1024,1,384]{2,1,0:T(1,128)} copy(f32[1024,1,384]{2,1,0:T(1,128)S(1)} %bitcast.2) | data formatting | bytes 3145728
Async XLA Ops:
  1.3 1.4 %copy-start = (f32[1024,1,384]{2,1,0:T(1,128)S(1)}, f32[1024,1,384]{2,1,0:T(1,128)}, u32[]{:S(2)}) copy-start(f32[1024,1,384]{2,1,0:T(1,128)} %param.4) | copy-start | bytes 4718596
  2.7 0.7 copy-start.1

commit v2 on v1

--- a/solution.py
+++ b/solution.py
@@ -14,6 +14,7 @@
 NQ = 1024
 V = 384
 QT = 256
+HALF = 3 * QT // 2
 OWNERS = 6
 
 
@@ -29,8 +30,8 @@
 
 
 def kernel(
-    own, occ, vir, mask, out,
-    nb, hp, lp, part, r1, r2, r3, r4, tot, amp, ah, al, acc, oc, vcol,
+    own, occ_hbm, vir_hbm, mask_hbm, out,
+    ow, occ, vir, mask, ls, nb, wide, part, r1, r2, r3, r4, tot, amp, fac, acc, oc, vcol, den, weight,
     bs, br, os_, or_, js, jr,
 ):
     y = lax.axis_index("pair")
@@ -61,8 +62,15 @@
     partners += [at_x(d) for d in (1, 2, 3)] + [at_z(d) for d in range(1, 8)] + [sibling]
     for partner in partners:
         pl.semaphore_signal(barrier, 1, device_id=partner, device_id_type=MESH)
+    local = [
+        pltpu.make_async_copy(src, dst, ls.at[i])
+        for i, (src, dst) in enumerate(((occ_hbm, occ), (vir_hbm, vir), (mask_hbm, mask), (own, ow)))
+    ]
+    for copy in local:
+        copy.start()
     pl.semaphore_wait(barrier, len(partners))
 
+    local[0].wait()
     oc[y] = jnp.full((8, 128), occ[0], f32)
     for i, t in enumerate((up, down, far)):
         remote(oc.at[y], oc.at[y], os_.at[i], or_.at[0], {"pair": t}).start()
@@ -75,15 +83,16 @@
             first, relay = wanted(y + 2), wanted(y + 1)
             src, dst, q = (
                 (own, 0, first), (own, 0, 1 - first), (nb.at[0], 2, relay),
-                (own, 0, 2), (own, 0, 3), (nb.at[0], 2, 1 - relay),
+                (own, 0, 2), (own, 0, 3), (nb.at[0], 2, 1 - relay), (own, 0, 3),
             )[k]
         else:
             first, relay = 2 + wanted(y + 2), 2 + wanted(y + 3)
             src, dst, q = (
                 (own, 1, first), (own, 1, 5 - first), (nb.at[1], 2, relay),
-                (own, 1, 0), (own, 1, 1), (nb.at[1], 2, 5 - relay),
+                (own, 1, 0), (own, 1, 1), (nb.at[1], 2, 5 - relay), (own, 1, 1),
             )[k]
-        rows = pl.ds(pl.multiple_of(q * (3 * QT), 8), 3 * QT)
+        skip, size = {4: (0, HALF), 6: (HALF, HALF)}.get(k, (0, 2 * HALF))
+        rows = pl.ds(pl.multiple_of(q * (2 * HALF) + skip, 8), size)
         return remote(
             src.at[rows], nb.at[dst, rows], bs.at[direction, k], br.at[direction, k],
             {"pair": up if direction == 0 else down},
@@ -102,12 +111,13 @@
         rows = pl.ds(pl.multiple_of(q * QT, QT), QT)
         for c in range(3):
             high, low = split(block[pl.ds(c, QT, stride=3), :])
-            hp[slot, rows, c * 128 : (c + 1) * 128] = high
-            lp[slot, rows, c * 128 : (c + 1) * 128] = low
+            for start, value in ((0, high), (V, low), (2 * V, high)):
+                wide[slot, rows, start + c * 128 : start + (c + 1) * 128] = value
 
     def contract(t, left, right, q, first):
         rows = pl.ds(pl.multiple_of(q * QT, QT), QT)
-        lh, ll, rh, rl = hp[left, rows], lp[left, rows], hp[right, rows], lp[right, rows]
+        lh, ll = wide[left, rows, 0:V], wide[left, rows, V : 2 * V]
+        rh, rl = wide[right, rows, 0:V], wide[right, rows, V : 2 * V]
         value = gram(lh, rh) + gram(lh, rl) + gram(ll, rh)
         part[t] = value if first else part[t] + value
 
@@ -115,7 +125,7 @@
     other = pl.multiple_of((1 - core) * 192, 8)
     mine_x = pl.multiple_of(half + x * 48, 8)
     mine = pl.multiple_of(mine_x + z * 8, 8)
-    jobs = {"D": (0, 0, 1), "E": (1, 1, 2), "F": (2, 3, 1)}
+    jobs = {"D": (0, 0, 1), "M": (1, 1, 1), "P": (2, 2, 1), "F": (3, 3, 1)}
     owner = z < OWNERS
 
     def core_sum(name, begin):
@@ -166,17 +176,14 @@
                 tot[b : b + n] = value
 
     def y_sum(name, begin):
-        j = jobs[name][0]
-        moves = {"E": ((1, 2, down, 3), (2, 1, up, 4)), "F": ((3, 3, far, 3),)}[name]
+        t, there, partner = {"M": (1, 2, down), "P": (2, 1, up), "F": (3, 3, far)}[name]
 
         @pl.when(owner)
         def _():
-            for src, dst, t, s in moves:
-                copy = remote(tot.at[src], r4.at[dst], js.at[j, s], jr.at[j, s], {"pair": t})
-                if begin:
-                    copy.start()
-                else:
-                    copy.wait_recv()
+            if begin:
+                remote(tot.at[t], r4.at[there], js.at[t, 3], jr.at[there, 3], {"pair": partner}).start()
+            else:
+                wait_bytes(r4.at[t], jr.at[t, 3])
 
     low_far = lax.rem(y, 2)
     sides = {0: (y, y), 1: (down, y), 2: (y, up), 3: (low_far, low_far + 2)}
@@ -187,11 +194,15 @@
         @pl.when(owner)
         def _():
             for t in range(b, b + n):
-                p, r = sides[t]
-                denominator = (vcol[pl.ds(mine, 8), 0:1] + vir[...]) - oc[p, 0:1, 0:1] - oc[r, 0:1, 0:1]
-                weight = mask[p, r].astype(f32)
                 total = tot[t] + r4[t] if t else tot[t]
-                amp[t, pl.ds(mine, 8)] = (weight * total) / denominator
+                amp[t, pl.ds(mine, 8)] = (weight[t, :, 0:1] * total) / den[t]
+
+    def prepare():
+        own_rows = pl.ds(pl.multiple_of(lax.rem(mine, V), 8), 8)
+        for t in range(4):
+            p, r = sides[t]
+            weight[t] = jnp.full((8, 128), mask[p, r].astype(f32))
+            den[t] = (vcol[own_rows, 0:1] + vir[...]) - oc[p, 0:1, 0:1] - oc[r, 0:1, 0:1]
 
     def z_gather(name, begin):
         j, b, n = jobs[name]
@@ -232,13 +243,13 @@
 
     def factor(slot, turned):
         value = amp[slot]
-        ah[slot], al[slot] = split(value.T if turned else value)
+        high, low = split(value.T if turned else value)
+        fac[slot, 0:V] = high
+        fac[slot, V : 2 * V] = high
+        fac[slot, 2 * V :] = low
 
     def back(slot, rows):
-        high = hp[slot, rows]
-        value = jnp.dot(high, ah[slot], preferred_element_type=f32)
-        value += jnp.dot(high, al[slot], preferred_element_type=f32)
-        return value + jnp.dot(lp[slot, rows], ah[slot], preferred_element_type=f32)
+        return jnp.dot(wide[slot, rows], fac[slot], preferred_element_type=f32)
 
     def quarters(body):
         def step(q, carry):
@@ -249,16 +260,31 @@
 
     q_far = wanted(y)
 
+    def own_step(q, rows):
+        convert(0, ow, q)
+        contract(0, 0, 0, q, False)
+
+    def own_back(q, rows):
+        acc[rows] = back(0, rows)
+
+    def up_back(q, rows):
+        acc[rows] += back(1, rows)
+
+    def down_back(q, rows):
+        acc[rows] += back(2, rows)
+
+    def far_back(q, rows):
+        value = acc[rows] + back(3, rows)
+        block = out.at[pl.ds(pl.multiple_of(q * (3 * QT), 8), 3 * QT)]
+        for c in range(3):
+            block[pl.ds(c, QT, stride=3), :] = value[:, c * 128 : (c + 1) * 128]
+
     send(0)
     send(1)
+    for copy in local[1:]:
+        copy.wait()
     vcol[...] = jnp.broadcast_to(vir[...], (128, V)).T
-
     part[0] = jnp.zeros((V, V), f32)
-
-    def own_step(q, rows):
-        convert(0, own, q)
-        contract(0, 0, 0, q, False)
-
     quarters(own_step)
     core_sum("D", True)
     wait_bytes(oc.at[pl.ds(0, 3)], or_.at[0])
@@ -266,86 +292,97 @@
     x_sum("D", True)
     arrive(0)
     send(2)
+    first_up, first_down = wanted(y + 1), 2 + wanted(y + 3)
+    convert(1, nb.at[0], first_up)
+    contract(1, 1, 0, first_up, True)
+    convert(2, nb.at[1], first_down)
+    contract(2, 0, 2, first_down, True)
+    prepare()
     x_sum("D", False)
     z_sum("D", True)
-    first_up, first_down = wanted(y + 1), 2 + wanted(y + 3)
-    convert(1, nb.at[0], first_up)
-    convert(2, nb.at[1], first_down)
-    contract(1, 1, 0, first_up, True)
-    contract(2, 0, 2, first_down, True)
     z_sum("D", False)
     scale("D")
     z_gather("D", True)
     arrive(1)
     send(3)
     convert(1, nb.at[0], 1 - first_up)
+    contract(1, 1, 0, 1 - first_up, False)
+    core_sum("M", True)
     convert(2, nb.at[1], 5 - first_down)
-    contract(1, 1, 0, 1 - first_up, False)
     contract(2, 0, 2, 5 - first_down, False)
-    core_sum("E", True)
+    core_sum("P", True)
+    core_sum("M", False)
+    x_sum("M", True)
+    core_sum("P", False)
+    x_sum("P", True)
     z_gather("D", False)
-    x_gather("D", True)
-    core_sum("E", False)
-    x_sum("E", True)
-    x_gather("D", False)
-    core_gather("D", True)
     arrive(2)
-    send(4)
+    left = jnp.where(y < 2, 0, 3)
     convert(3, nb.at[2], q_far)
+    contract(3, left, 3 - left, q_far, True)
     convert(3, nb.at[2], 2 + q_far)
-    left = jnp.where(y < 2, 0, 3)
-    contract(3, left, 3 - left, q_far, True)
     contract(3, left, 3 - left, 2 + q_far, False)
     core_sum("F", True)
-    x_sum("E", False)
-    z_sum("E", True)
+    x_sum("M", False)
+    z_sum("M", True)
     core_sum("F", False)
     x_sum("F", True)
-    core_gather("D", False)
-    factor(0, False)
-
-    def own_back(q, rows):
-        acc[rows] = back(0, rows)
-
-    quarters(own_back)
-    z_sum("E", False)
-    y_sum("E", True)
+    x_sum("P", False)
+    z_sum("P", True)
+    x_gather("D", True)
+    z_sum("M", False)
+    y_sum("M", True)
+    send(4)
     x_sum("F", False)
     z_sum("F", True)
+    z_sum("P", False)
+    y_sum("P", True)
+    y_sum("M", False)
+    scale("M")
+    z_gather("M", True)
     arrive(3)
     convert(1, nb.at[0], 2)
     convert(2, nb.at[1], 0)
-    y_sum("E", False)
-    scale("E")
-    z_gather("E", True)
     z_sum("F", False)
     y_sum("F", True)
+    send(6)
     send(5)
-    arrive(4)
-    convert(1, nb.at[0], 3)
-    convert(2, nb.at[1], 1)
+    y_sum("P", False)
+    scale("P")
+    z_gather("P", True)
+    z_gather("M", False)
+    x_gather("M", True)
     y_sum("F", False)
     scale("F")
     z_gather("F", True)
-    z_gather("E", False)
-    x_gather("E", True)
+    x_gather("D", False)
+    core_gather("D", True)
+    z_gather("P", False)
+    x_gather("P", True)
+    core_gather("D", False)
+    factor(0, False)
+    quarters(own_back)
     z_gather("F", False)
     x_gather("F", True)
-    x_gather("E", False)
-    core_gather("E", True)
+    arrive(4)
+    arrive(6)
+    convert(1, nb.at[0], 3)
+    convert(2, nb.at[1], 1)
+    x_gather("M", False)
+    core_gather("M", True)
+    core_gather("M", False)
+    factor(1, False)
+    x_gather("P", False)
+    core_gather("P", True)
+    quarters(up_back)
+    core_gather("P", False)
+    factor(2, True)
+    x_gather("F", False)
+    core_gather("F", True)
+    quarters(down_back)
     arrive(5)
     convert(3, nb.at[2], 1 - q_far)
     convert(3, nb.at[2], 3 - q_far)
-    core_gather("E", False)
-    factor(1, False)
-    factor(2, True)
-
-    def near_back(q, rows):
-        acc[rows] += back(1, rows) + back(2, rows)
-
-    quarters(near_back)
-    x_gather("F", False)
-    core_gather("F", True)
     core_gather("F", False)
 
     @pl.when(y < 2)
@@ -356,15 +393,9 @@
     def _():
         factor(3, False)
 
-    def far_back(q, rows):
-        value = acc[rows] + back(3, rows)
-        block = out.at[pl.ds(pl.multiple_of(q * (3 * QT), 8), 3 * QT)]
-        for c in range(3):
-            block[pl.ds(c, QT, stride=3), :] = value[:, c * 128 : (c + 1) * 128]
-
     quarters(far_back)
 
-    for k in range(6):
+    for k in range(7):
         for d in (0, 1):
             bulk(k, d).wait_send()
     for i in range(3):
@@ -380,8 +411,8 @@
         def _():
             wait_bytes(r3.at[pl.ds(0, OWNERS - 1), blocks], js.at[j, 2])
             wait_bytes(r3.at[:, blocks], js.at[j, 5])
-            for s in range(3, 3 + {"D": 0, "E": 2, "F": 1}[name]):
-                wait_bytes(tot.at[0], js.at[j, s])
+            if name != "D":
+                wait_bytes(tot.at[0], js.at[j, 3])
 
         @pl.when(jnp.logical_not(owner))
         def _():
@@ -391,17 +422,21 @@
 def on_device(three_center, occ_energy, vir_energy, pair_mask):
     flat = three_center.reshape(3 * NQ, 128)
     vmem = pl.BlockSpec(memory_space=pltpu.VMEM)
-    smem = pl.BlockSpec(memory_space=pltpu.SMEM)
+    hbm = pl.BlockSpec(memory_space=pltpu.HBM)
     dma = pltpu.SemaphoreType.DMA
     result = pl.pallas_call(
         kernel,
         out_shape=jax.ShapeDtypeStruct((3 * NQ, 128), f32),
-        in_specs=[vmem, smem, vmem, smem],
+        in_specs=[hbm] * 4,
         out_specs=vmem,
         scratch_shapes=[
+            pltpu.VMEM((3 * NQ, 128), f32),
+            pltpu.SMEM((1,), f32),
+            pltpu.VMEM((1, V), f32),
+            pltpu.SMEM((4, 4), jnp.int32),
+            dma((4,)),
             pltpu.VMEM((3, 3 * NQ, 128), f32),
-            pltpu.VMEM((4, NQ, V), bf16),
-            pltpu.VMEM((4, NQ, V), bf16),
+            pltpu.VMEM((4, NQ, 3 * V), bf16),
             pltpu.VMEM((4, V, V), f32),
             pltpu.VMEM((4, 192, V), f32),
             pltpu.VMEM((3, 4, 48, V), f32),
@@ -409,20 +444,21 @@
             pltpu.VMEM((4, 8, V), f32),
             pltpu.VMEM((4, 8, V), f32),
             pltpu.VMEM((4, V, V), f32),
-            pltpu.VMEM((4, V, V), bf16),
-            pltpu.VMEM((4, V, V), bf16),
+            pltpu.VMEM((4, 3 * V, V), bf16),
             pltpu.VMEM((NQ, V), f32),
             pltpu.VMEM((4, 8, 128), f32),
             pltpu.VMEM((V, 128), f32),
-            dma((2, 6)),
-            dma((2, 6)),
+            pltpu.VMEM((4, 8, V), f32),
+            pltpu.VMEM((4, 8, 128), f32),
+            dma((2, 7)),
+            dma((2, 7)),
             dma((3,)),
             dma((1,)),
-            dma((3, 8)),
-            dma((3, 8)),
+            dma((4, 8)),
+            dma((4, 8)),
         ],
         compiler_params=pltpu.CompilerParams(
-            collective_id=0, has_side_effects=True, vmem_limit_bytes=48 << 20
+            collective_id=0, has_side_effects=True, vmem_limit_bytes=52 << 20
         ),
     )(flat, occ_energy, vir_energy.reshape(1, V), pair_mask)
     return result.reshape(NQ, 1, V)

time: 83.5 us -> 74.2 us (0.89)
  Pallas kernels: 78.8 us -> 70.9 us
  local copies, waits for them, and re-layouts: 3.92 us -> 2.51 us
    pallas_call x1, Pallas kernels: 78.8 us -> 70.9 us  [on_device(): pl.pallas_call(kernel, out_shape=jax.ShapeDtypeStruct((3 * NQ, 128), f32)...]
    unnamed x5 -> x3, local copies, waits for them, and re-layouts: 3.23 us -> 1.83 us
where the time goes in v2:
time: 74.2 us; the launch traced here: 74.1 us
  Pallas kernels  70.9 us (96%)
  local copies, waits for them, and re-layouts  2.51 us (3%)
    pallas_call x1, Pallas kernels, on_device(): pl.pallas_call(kernel, out_shape=jax.ShapeDtypeStruct((3 * NQ, 128), f32)...  70.9 us
    unnamed x3, local copies, waits for them, and re-layouts  1.83 us

profile of v2, /device:TPU:1, one launch (start us, length us, event | category | flops | bytes accessed | tf_op | source)
XLA Modules:
  0.0 74.1 jit_solution(987534201557178141)
XLA Ops:
  0.7 0.7 reshape.10.vir_hbm
  1.3 0.0 copy-start
  1.3 0.7 copy-done
  2.0 70.9 %shard_map.46 = f32[3072,128]{1,0:T(8,128)S(1)} custom-call(f32[3072,128]{1,0:T(8,128)} %bitcast.3, f32[1]{0:T(128)S(6)} %copy.7.occ_hbm, f32[1,384]{1,0:T(1,128)S(1)} %reshape.10.vir_hbm, s32[4,4]{1,0:T(4,128)S(1)} %copy-done), custom_call_target="tpu_custom_call" | custom-call | tf_op jit(solution)/shard_map/pallas_call | solution.py:427
  73.0 1.1 %copy.8 = f32[1024,1,384]{2,1,0:T(1,128)} copy(f32[1024,1,384]{2,1,0:T(1,128)S(1)} %bitcast.2) | data formatting | bytes 3145728
Async XLA Ops:
  1.3 0.7 copy-start

commit v3 on v2

--- a/solution.py
+++ b/solution.py
@@ -58,8 +58,8 @@
         pltpu.make_async_copy(ref, ref, sem).wait()
 
     barrier = pltpu.get_barrier_semaphore()
-    partners = [{"pair": t} for t in (up, down, far)]
-    partners += [at_x(d) for d in (1, 2, 3)] + [at_z(d) for d in range(1, 8)] + [sibling]
+    partners = [at_z(d) for d in (4, 3, 5, 2, 6, 1, 7)]
+    partners += [{"pair": t} for t in (far, up, down)] + [at_x(d) for d in (2, 1, 3)] + [sibling]
     for partner in partners:
         pl.semaphore_signal(barrier, 1, device_id=partner, device_id_type=MESH)
     local = [
@@ -69,11 +69,6 @@
     for copy in local:
         copy.start()
     pl.semaphore_wait(barrier, len(partners))
-
-    local[0].wait()
-    oc[y] = jnp.full((8, 128), occ[0], f32)
-    for i, t in enumerate((up, down, far)):
-        remote(oc.at[y], oc.at[y], os_.at[i], or_.at[0], {"pair": t}).start()
 
     def wanted(node):
         return lax.rem(node, 4) // 2
@@ -251,12 +246,12 @@
     def back(slot, rows):
         return jnp.dot(wide[slot, rows], fac[slot], preferred_element_type=f32)
 
-    def quarters(body):
+    def quarters(body, low=0, high=4):
         def step(q, carry):
             body(q, pl.ds(pl.multiple_of(q * QT, QT), QT))
             return carry
 
-        lax.fori_loop(0, 4, step, 0)
+        lax.fori_loop(low, high, step, 0)
 
     q_far = wanted(y)
 
@@ -279,6 +274,10 @@
         for c in range(3):
             block[pl.ds(c, QT, stride=3), :] = value[:, c * 128 : (c + 1) * 128]
 
+    local[0].wait()
+    oc[y] = jnp.full((8, 128), occ[0], f32)
+    for i, t in enumerate((up, down, far)):
+        remote(oc.at[y], oc.at[y], os_.at[i], or_.at[0], {"pair": t}).start()
     send(0)
     send(1)
     for copy in local[1:]:
@@ -287,7 +286,6 @@
     part[0] = jnp.zeros((V, V), f32)
     quarters(own_step)
     core_sum("D", True)
-    wait_bytes(oc.at[pl.ds(0, 3)], or_.at[0])
     core_sum("D", False)
     x_sum("D", True)
     arrive(0)
@@ -297,6 +295,7 @@
     contract(1, 1, 0, first_up, True)
     convert(2, nb.at[1], first_down)
     contract(2, 0, 2, first_down, True)
+    wait_bytes(oc.at[pl.ds(0, 3)], or_.at[0])
     prepare()
     x_sum("D", False)
     z_sum("D", True)
@@ -329,12 +328,12 @@
     x_sum("F", True)
     x_sum("P", False)
     z_sum("P", True)
-    x_gather("D", True)
     z_sum("M", False)
     y_sum("M", True)
     send(4)
     x_sum("F", False)
     z_sum("F", True)
+    x_gather("D", True)
     z_sum("P", False)
     y_sum("P", True)
     y_sum("M", False)
@@ -350,11 +349,11 @@
     y_sum("P", False)
     scale("P")
     z_gather("P", True)
-    z_gather("M", False)
-    x_gather("M", True)
     y_sum("F", False)
     scale("F")
     z_gather("F", True)
+    z_gather("M", False)
+    x_gather("M", True)
     x_gather("D", False)
     core_gather("D", True)
     z_gather("P", False)
@@ -367,19 +366,21 @@
     arrive(4)
     arrive(6)
     convert(1, nb.at[0], 3)
-    convert(2, nb.at[1], 1)
     x_gather("M", False)
     core_gather("M", True)
+    convert(2, nb.at[1], 1)
     core_gather("M", False)
     factor(1, False)
+    quarters(up_back, 0, 2)
     x_gather("P", False)
     core_gather("P", True)
-    quarters(up_back)
+    quarters(up_back, 2, 4)
     core_gather("P", False)
     factor(2, True)
+    quarters(down_back, 0, 2)
     x_gather("F", False)
     core_gather("F", True)
-    quarters(down_back)
+    quarters(down_back, 2, 4)
     arrive(5)
     convert(3, nb.at[2], 1 - q_far)
     convert(3, nb.at[2], 3 - q_far)

time: 74.2 us -> 74 us (level)
  no operation moved by 1% of the time
where the time goes in v3:
time: 74 us; the launch traced here: 73.9 us
  Pallas kernels  70.7 us (96%)
  local copies, waits for them, and re-layouts  2.51 us (3%)
    pallas_call x1, Pallas kernels, on_device(): pl.pallas_call(kernel, out_shape=jax.ShapeDtypeStruct((3 * NQ, 128), f32)...  70.7 us
    unnamed x3, local copies, waits for them, and re-layouts  1.83 us

profile of v3, /device:TPU:1, one launch (start us, length us, event | category | flops | bytes accessed | tf_op | source)
XLA Modules:
  0.0 73.9 jit_solution(15248953990327029838)
XLA Ops:
  0.7 0.7 reshape.10.vir_hbm
  1.3 0.0 copy-start
  1.3 0.7 copy-done
  2.0 70.7 %shard_map.46 = f32[3072,128]{1,0:T(8,128)S(1)} custom-call(f32[3072,128]{1,0:T(8,128)} %bitcast.3, f32[1]{0:T(128)S(6)} %copy.7.occ_hbm, f32[1,384]{1,0:T(1,128)S(1)} %reshape.10.vir_hbm, s32[4,4]{1,0:T(4,128)S(1)} %copy-done), custom_call_target="tpu_custom_call" | custom-call | tf_op jit(solution)/shard_map/pallas_call | solution.py:428
  72.7 1.1 %copy.8 = f32[1024,1,384]{2,1,0:T(1,128)} copy(f32[1024,1,384]{2,1,0:T(1,128)S(1)} %bitcast.2) | data formatting | bytes 3145728
Async XLA Ops:
  1.3 0.7 copy-start
